TPU v7x, 32 devices: a whole 2x2x4 slice. The times are simulated.
32 devices in a mesh: dp: 2 (over x), seq: 16 (over z, y, core).
Axes of the slice: x: 2, y: 2, z: 4, core: 2. Of those that a mesh axis runs over, the one named last changes fastest.
Arguments:
- inputs: bfloat16 [64, 256, 1024], P('seq', 'dp'), may hold values from -6 to 6
- gates: bfloat16 [64, 256, 1024], P('seq', 'dp'), may hold values from -6 to 6
- kernel: bfloat16 [64, 256, 1024], P('seq', 'dp'), may hold values from -5 to 5
- first_factor: bfloat16 [1024, 1024], replicated, may hold values from -0.1875 to 0.1875
- second_factor: bfloat16 [64, 64], replicated, may hold values from -0.75 to 0.75
- upstream: bfloat16 [64, 256, 1024], P('seq', 'dp'), may hold values from -6 to 6
Outputs:
- output: bfloat16 [64, 256, 1024], P('seq', 'dp')
- grad_inputs: bfloat16 [64, 256, 1024], P('seq', 'dp')
- grad_gates: bfloat16 [64, 256, 1024], P('seq', 'dp')
- grad_kernel: bfloat16 [64, 256, 1024], P('seq', 'dp')
- grad_first: float32 [1024, 1024], P('seq')
- grad_second: float32 [64, 64], P('seq')
All inputs are finite; a program needn't handle non-finite values.
Results may differ from a plain program's by a relative error of at most 0.0065.
Values may be sent and summed in bfloat16 or wider, within the bound.
A program may use at most 64 MiB of HBM per device.

v0:
```python
import math

import jax
import jax.numpy as jnp
from jax import lax
from jax.sharding import PartitionSpec as P


def on_device(inputs, gates, kernel, first_factor, second_factor, upstream):
    local_blocks, channels, width = inputs.shape
    seq_count = lax.axis_size("seq")
    all_channels = channels * lax.axis_size("dp")
    sig = jax.nn.sigmoid(gates.astype(jnp.float32))
    mixed_in = (inputs.astype(jnp.float32) * sig).astype(jnp.bfloat16)
    flat_in = mixed_in.reshape(local_blocks * channels, width)
    blocks = lax.dot_general(
        flat_in, first_factor, (((1,), (1,)), ((), ())), preferred_element_type=jnp.float32
    )
    blocks = blocks.astype(jnp.bfloat16).reshape(local_blocks, channels, width)
    kerneled = (blocks.astype(jnp.float32) * kernel.astype(jnp.float32)).astype(jnp.bfloat16)
    kern_rows = kerneled.reshape(local_blocks, channels * width)
    up_rows = upstream.reshape(local_blocks, channels * width)
    flat_moved = lax.all_to_all(kern_rows, "seq", split_axis=1, concat_axis=0, tiled=True)
    all_blocks = flat_moved.shape[0]
    across = jnp.dot(second_factor, flat_moved, preferred_element_type=jnp.float32).astype(
        jnp.bfloat16
    )
    output = lax.all_to_all(across, "seq", split_axis=0, concat_axis=1, tiled=True).reshape(
        local_blocks, channels, width
    )
    flat_up = lax.all_to_all(up_rows, "seq", split_axis=1, concat_axis=0, tiled=True)
    grad_across = lax.dot_general(
        second_factor, flat_up, (((0,), (0,)), ((), ())), preferred_element_type=jnp.float32
    )
    grad_across = grad_across.astype(jnp.bfloat16)
    grad_mid = lax.all_to_all(grad_across, "seq", split_axis=0, concat_axis=1, tiled=True).reshape(
        local_blocks, channels, width
    )
    grad_kernel = (grad_mid.astype(jnp.float32) * blocks.astype(jnp.float32)).astype(jnp.bfloat16)
    grad_blocks = (grad_mid.astype(jnp.float32) * kernel.astype(jnp.float32)).astype(jnp.bfloat16)
    flat_grad = grad_blocks.reshape(local_blocks * channels, width)
    grad_mixed = jnp.dot(flat_grad, first_factor, preferred_element_type=jnp.float32).reshape(
        local_blocks, channels, width
    )
    grad_inputs = (grad_mixed * sig).astype(jnp.bfloat16)
    grad_gates = (grad_mixed * inputs.astype(jnp.float32) * sig * (1.0 - sig)).astype(jnp.bfloat16)
    first_norm = 1.0 / math.sqrt(all_blocks * all_channels)
    second_norm = 1.0 / math.sqrt(all_channels * width)
    first_owned = width // seq_count
    second_owned = all_blocks // seq_count
    first_full = lax.dot_general(
        flat_grad, flat_in, (((0,), (0,)), ((), ())), preferred_element_type=jnp.float32
    )
    second_full = lax.dot_general(
        flat_up, flat_moved, (((1,), (1,)), ((), ())), preferred_element_type=jnp.float32
    )
    first_total, second_total = lax.psum((first_full, second_full), ("dp", "seq"))
    position = lax.axis_index("seq")
    first_sum = lax.dynamic_slice_in_dim(first_total, position * first_owned, first_owned, 0)
    second_sum = lax.dynamic_slice_in_dim(second_total, position * second_owned, second_owned, 0)
    grad_first = first_sum * first_norm
    grad_second = second_sum * second_norm
    return (output, grad_inputs, grad_gates, grad_kernel, grad_first, grad_second)


def solution(mesh):
    in_specs = (
        P("seq", "dp", None),
        P("seq", "dp", None),
        P("seq", "dp", None),
        P(),
        P(),
        P("seq", "dp", None),
    )
    out_specs = (
        P("seq", "dp", None),
        P("seq", "dp", None),
        P("seq", "dp", None),
        P("seq", "dp", None),
        P("seq", None),
        P("seq", None),
    )
    return jax.shard_map(
        on_device, mesh=mesh, in_specs=in_specs, out_specs=out_specs, check_vma=False
    )
```

profile of v0, /device:TPU:0, one launch (start us, length us, event | category | flops | bytes accessed | tf_op | source)
XLA Modules:
  0.0 281.6 jit_solution(2887516587283817598)
XLA Ops:
  7.2 2.5 all_to_all.57
  9.7 2.0 copy.18
  11.7 32.1 %all_to_all.67 = bf16[4,16,8192]{2,0,1:T(4,128)(2,1)} all-to-all(bf16[4,16,8192]{2,0,1:T(4,128)(2,1)S(1)} %copy.18), channel_id=1, replica_groups=mesh['dp'=2,'seq'=16] {'seq'}, dimensions={1} | all-to-all | bytes 2097152 | tf_op jit(solution)/shard_map/all_to_all | solution.py:31
  45.2 1.4 convolution_convert_fusion.1
  46.6 2.2 all_to_all.61
  48.9 29.8 %all_to_all.68 = bf16[16,4,8192]{2,1,0:T(4,128)(2,1)S(1)} all-to-all(bf16[16,4,8192]{2,1,0:T(4,128)(2,1)} %all_to_all.61), channel_id=1, replica_groups=mesh['dp'=2,'seq'=16] {'seq'}, dimensions={0} | all-to-all | bytes 2097152 | tf_op jit(solution)/shard_map/all_to_all | solution.py:36
  78.9 2.6 copy.19
  81.5 2.7 reshape.49
  84.2 5.7 %fusion.4 = (bf16[4,128,1024]{2,1,0:T(8,128)(2,1)}, bf16[4,128,1024]{2,1,0:T(8,128)(2,1)}, bf16[4,128,1024]{2,1,0:T(8,128)(2,1)S(1)}) fusion(bf16[4,128,1024]{2,1,0:T(8,128)(2,1)} %param.6, bf16[4,128,1024]{2,1,0:T(8,128)(2,1)} %param.7, bf16[1024,1024]{1,0:T(8,128)(2,1)S(1)} %copy-done, f32[4,128,1024]{2,1,0:T(8,128)} %reshape.49, ...), kind=kOutput, calls=%fused_computation.12 | convolution fusion | flops 1082654720 | bytes 10485760 | tf_op jit(solution)/shard_map/dot_general | solution.py:42
  92.1 2.0 fusion.7
  94.1 2.3 all_to_all.50
  96.4 3.0 %copy.16 = bf16[4,16,8192]{2,0,1:T(4,128)(2,1)} copy(bf16[4,16,8192]{2,1,0:T(8,128)(2,1)} %all_to_all.50) | data formatting | bytes 2097152 | tf_op jit(solution)/shard_map/all_to_all | solution.py:23
  99.4 5.0 %all-to-all-start = ((bf16[4,16,8192]{2,0,1:T(4,128)(2,1)}), bf16[4,16,8192]{2,0,1:T(4,128)(2,1)}, u32[]{:S(2)}, u32[]{:S(2)}) async-start(bf16[4,16,8192]{2,0,1:T(4,128)(2,1)} %copy.16), calls=%async_computation | async-start | bytes 2097152 | tf_op jit(solution)/shard_map/all_to_all | solution.py:23
  104.5 5.4 %convolution_bitcast_fusion = f32[1024,1024]{1,0:T(8,128)} fusion(bf16[4,128,1024]{2,1,0:T(8,128)(2,1)} %copy-done.3, f32[4,128,1024]{2,1,0:T(8,128)} %reshape.49, bf16[4,128,1024]{2,1,0:T(8,128)(2,1)} %param.8), kind=kOutput, calls=%fused_computation.8 | convolution fusion | flops 1075314688 | bytes 8388608 | tf_op jit(solution)/shard_map/dot_general | solution.py:51
  110.0 22.6 %all-to-all-done = bf16[4,16,8192]{2,0,1:T(4,128)(2,1)} async-done(((bf16[4,16,8192]{2,0,1:T(4,128)(2,1)}), bf16[4,16,8192]{2,0,1:T(4,128)(2,1)}, u32[]{:S(2)}, u32[]{:S(2)}) %all-to-all-start) | async-done | bytes 1048608 | tf_op jit(solution)/shard_map/all_to_all | solution.py:23
  132.6 2.1 all_to_all.53
  134.7 2.6 fusion
  137.4 2.3 all_to_all.54
  139.7 8.8 %all-to-all-start.1 = ((bf16[16,4,8192]{2,1,0:T(4,128)(2,1)}), bf16[16,4,8192]{2,1,0:T(4,128)(2,1)}, u32[]{:S(2)}, u32[]{:S(2)}) async-start(bf16[16,4,8192]{2,1,0:T(4,128)(2,1)} %all_to_all.54), calls=%async_computation.1 | async-start | bytes 2097152 | tf_op jit(solution)/shard_map/all_to_all | solution.py:28
  148.5 1.7 convolution_bitcast_fusion.1
  150.2 50.0 %psum.15 = f32[64,64]{0,1:T(8,128)S(1)} all-reduce(f32[64,64]{0,1:T(8,128)S(1)} %convolution_bitcast_fusion.1), channel_id=1, replica_groups=mesh['dp'=2,'seq'=16] {'dp','seq'}, use_global_device_ids=true, to_apply=%region_1.0 | all-reduce | flops 4096 | bytes 32768 | tf_op jit(solution)/shard_map/psum | solution.py:57
  200.9 69.0 %all-reduce.2.cloned.1.call-done = f32[1024,1024]{1,0:T(8,128)} async-done(((f32[1024,1024]{1,0:T(8,128)}), f32[1024,1024]{1,0:T(8,128)}) %all-reduce.2.cloned.1.call-update) | async-done | bytes 4194320 | tf_op jit(solution)/shard_map/psum | solution.py:57
  270.0 1.7 dynamic-slice_multiply_fusion
  271.7 1.8 copy.17
  (19 shorter events, 5.9 us)
Async XLA Ops:
  7.2 77.1 %copy-start = (bf16[1024,1024]{1,0:T(8,128)(2,1)S(1)}, bf16[1024,1024]{1,0:T(8,128)(2,1)}, u32[]{:S(2)}) copy-start(bf16[1024,1024]{1,0:T(8,128)(2,1)} %param.9) | copy-start | bytes 6291460
  11.7 33.5 %copy-start.4 = (bf16[64,64]{1,0:T(8,128)(2,1)S(1)}, bf16[64,64]{1,0:T(8,128)(2,1)}, u32[]{:S(2)}) copy-start(bf16[64,64]{1,0:T(8,128)(2,1)} %param.10) | copy-start | bytes 24580
  89.9 1.3 copy-start.3
  89.9 2.0 copy-start.1
  89.9 2.2 copy-start.2
  99.4 33.2 %all-to-all-start = ((bf16[4,16,8192]{2,0,1:T(4,128)(2,1)}), bf16[4,16,8192]{2,0,1:T(4,128)(2,1)}, u32[]{:S(2)}, u32[]{:S(2)}) async-start(bf16[4,16,8192]{2,0,1:T(4,128)(2,1)} %copy.16), calls=%async_computation | async-start | bytes 2097152 | tf_op jit(solution)/shard_map/all_to_all | solution.py:23
  104.5 165.5 %all-reduce.2.cloned.1.call-start = ((), (), s32[]{:S(2)}) async-start(), calls=%async_computation.4 | async-start | bytes 8388608 | tf_op jit(solution)/shard_map/psum | solution.py:57
  139.7 132.0 %all-to-all-start.1 = ((bf16[16,4,8192]{2,1,0:T(4,128)(2,1)}), bf16[16,4,8192]{2,1,0:T(4,128)(2,1)}, u32[]{:S(2)}, u32[]{:S(2)}) async-start(bf16[16,4,8192]{2,1,0:T(4,128)(2,1)} %all_to_all.54), calls=%async_computation.1 | async-start | bytes 2097152 | tf_op jit(solution)/shard_map/all_to_all | solution.py:28
Sparse Core Ops, SparseCore 0:
  110.9 159.0 all-reduce.1
where the time goes:
time: 282 us
  blocking collectives  112 us (40%)
  waiting for transfers between devices  91.7 us (33%)
  local copies, waits for them, and re-layouts  27.9 us (10%)
  matrix products  18.1 us (6%)
  between operations  14.1 us (5%)
  starting transfers between devices  13.9 us (5%)
  other arithmetic  3.93 us (1%)
    psum x1, waiting for transfers between devices, on_device(): lax.psum((first_full, second_full), ('dp', 'seq'))  69 us
    psum x1, blocking collectives, on_device(): lax.psum((first_full, second_full), ('dp', 'seq'))  50 us
    all_to_all x1, blocking collectives, on_device(): lax.all_to_all(up_rows, 'seq', split_axis=1, concat_axis=0, tiled=True)  32.1 us
    all_to_all x1, blocking collectives, on_device(): lax.all_to_all(grad_across, 'seq', split_axis=0, concat_axis=1, tiled=True)  29.8 us
    all_to_all x1, waiting for transfers between devices, on_device(): lax.all_to_all(kern_rows, 'seq', split_axis=1, concat_axis=0, tiled=True)  22.6 us
    all_to_all x1, starting transfers between devices, on_device(): lax.all_to_all(across, 'seq', split_axis=0, concat_axis=1, tiled=True)  8.83 us
    all_to_all x3, local copies, waits for them, and re-layouts, on_device(): lax.all_to_all(kern_rows, 'seq', split_axis=1, concat_axis=0, tiled=True)  7.47 us
    all_to_all x3, local copies, waits for them, and re-layouts, on_device(): lax.all_to_all(up_rows, 'seq', split_axis=1, concat_axis=0, tiled=True)  5.85 us
  transfers between devices with their start and end apart: 3, of which 2 were waited for; matrix products, arithmetic and copies ran while one was open for 4% of the time, Pallas kernels for 0%

commit v1 on v0

v1 whole, which is shorter than its diff:
```python
import functools
import math

import jax
import jax.numpy as jnp
from jax import lax
from jax.experimental import pallas as pl
from jax.experimental.pallas import tpu as pltpu
from jax.sharding import PartitionSpec as P

MESH = pl.DeviceIdType.MESH
BF = jnp.bfloat16
F32 = jnp.float32
CS = 16


def dot(a, b, ca, cb, **kw):
    return lax.dot_general(a, b, (((ca,), (cb,)), ((), ())), preferred_element_type=F32, **kw)


def layer_kernel(
    n, dps, lb, ch, w, nb,
    x_hbm, g_hbm, k_hbm, f_hbm, s_ref, u_hbm,
    out_hbm, gi_hbm, gg_hbm, gk_hbm, gf_ref, gs_ref,
    x, g, k, f, mixed, blocks, kern, mu, mk, gac, oac, gm, om, gb, gi, gg, gk,
    kron, kron_t, gf, rs_send, rs_recv, dpbuf, g2s, g2r, g2dp,
    load_sem, own_sem, store_sem, send_sem, recv_sem, rs_ssem, rs_rsem,
    g2_ssem, g2_rsem, dp_ssem, dp_rsem,
):
    me = lax.axis_index("seq")
    my_dp = lax.axis_index("dp")
    pg = n // (ch // CS)
    pw = w // pg
    rows = nb * CS
    step_rows = 4 * lb * CS
    steps = n // 4
    owned = w // n
    levels = n.bit_length() - 1

    def share(ref, d):
        c0 = pl.multiple_of(lax.div(d, pg) * CS, CS)
        p0 = pl.multiple_of(lax.rem(d, pg) * pw, pw)
        return ref.at[:, pl.ds(c0, CS), pl.ds(p0, pw)]

    def part(ref, d):
        return ref.at[pl.ds(d * lb, lb)]

    def copy_to(phase, src, dst, d, s):
        return pltpu.make_async_remote_copy(
            src_ref=src, dst_ref=dst,
            send_sem=send_sem.at[phase, d], recv_sem=recv_sem.at[phase, s],
            device_id={"seq": d}, device_id_type=MESH,
        )

    loads = [
        pltpu.make_async_copy(a, b, load_sem.at[i])
        for i, (a, b) in enumerate(((g_hbm, g), (x_hbm, x), (f_hbm, f), (k_hbm, k)))
    ]
    for c in loads:
        c.start()
    own_u = pltpu.make_async_copy(share(u_hbm, me), part(mu, me), own_sem.at[0])
    own_u.start()

    barrier = pltpu.get_barrier_semaphore()

    @pl.loop(1, n)
    def _(j):
        pl.semaphore_signal(
            barrier, inc=1, device_id={"seq": lax.rem(me + j, n)}, device_id_type=MESH
        )

    for j in range(1, dps):
        pl.semaphore_signal(
            barrier, inc=1, device_id={"dp": lax.rem(my_dp + j, dps)}, device_id_type=MESH
        )
    pl.semaphore_wait(barrier, n - 1 + dps - 1)

    @pl.loop(1, n)
    def _(j):
        d = lax.rem(me + j, n)
        copy_to(0, share(u_hbm, d), part(mu, me), d, me).start()

    for c in loads:
        c.wait()

    @pl.loop(0, lb)
    def _(i):
        sig = jax.nn.sigmoid(g[i].astype(F32))
        mixed[i] = (x[i].astype(F32) * sig).astype(BF)

    @pl.loop(0, w // 256)
    def _(j):
        cols = pl.ds(pl.multiple_of(j * 256, 256), 256)
        b = dot(mixed[...].reshape(lb * ch, w), f[cols, :], 1, 1)
        b = b.astype(BF).reshape(lb, ch, 256)
        blocks[:, :, cols] = b
        kern[:, :, cols] = (b.astype(F32) * k[:, :, cols].astype(F32)).astype(BF)

    def spread(r0, count, width):
        r = lax.broadcasted_iota(jnp.int32, (count, width), 0) + r0
        lo = lax.broadcasted_iota(jnp.int32, (count, width), 1) * CS
        return jnp.where((r >= lo) & (r < lo + CS), 1.0, 0.0)

    def same_channel():
        r = lax.broadcasted_iota(jnp.int32, (step_rows, rows), 0)
        c = lax.broadcasted_iota(jnp.int32, (step_rows, rows), 1)
        return (r & (CS - 1)) == (c & (CS - 1))

    def build(dst, dim):
        @pl.loop(0, steps)
        def _(j):
            r0 = pl.multiple_of(j * step_rows, step_rows)
            a = dot(spread(r0, step_rows, nb).astype(BF), s_ref[...], 1, dim).astype(BF)
            e = dot(a, spread(0, rows, nb).astype(BF), 1, 1)
            dst[pl.ds(r0, step_rows), :] = jnp.where(same_channel(), e, 0.0).astype(BF)

    build(kron_t, 1)
    build(kron, 0)

    def wait_in(phase, dst):
        @pl.loop(1, n)
        def _(j):
            s = lax.rem(me + j, n)
            copy_to(phase, part(dst, s), part(dst, s), s, s).wait_recv()

    def wait_back(phase, dst):
        @pl.loop(1, n)
        def _(j):
            s = lax.rem(me + j, n)
            copy_to(phase, share(dst, s), share(dst, s), s, s).wait_recv()

    def mix(phase, matrix, src, acc, dst, sem):
        @pl.loop(0, steps)
        def _(j):
            at = lax.rem(lax.div(me, 4) + j, steps)
            r0 = pl.multiple_of(at * step_rows, step_rows)
            res = dot(matrix[pl.ds(r0, step_rows), :], src[...].reshape(rows, pw), 1, 0)
            acc[pl.ds(at * 4 * lb, 4 * lb)] = res.astype(BF).reshape(4 * lb, CS, pw)

            @pl.loop(0, 4)
            def _(i):
                d = at * 4 + i

                @pl.when(d != me)
                def _():
                    copy_to(phase, part(acc, d), share(dst, me), d, me).start()

        own = pltpu.make_async_copy(part(acc, me), share(dst, me), sem)
        own.start()
        return own

    own_u.wait()
    wait_in(0, mu)
    own_g = mix(1, kron_t, mu, gac, gm, own_sem.at[1])

    own_k = pltpu.make_async_copy(share(kern, me), part(mk, me), own_sem.at[2])
    own_k.start()

    @pl.loop(1, n)
    def _(j):
        d = lax.rem(me + j, n)
        copy_to(2, share(kern, d), part(mk, me), d, me).start()

    own_g.wait()
    wait_back(1, gm)

    @pl.loop(0, lb)
    def _(i):
        mid = gm[i].astype(F32)
        gk[i] = (mid * blocks[i].astype(F32)).astype(BF)
        gb[i] = (mid * k[i].astype(F32)).astype(BF)

    gk_store = pltpu.make_async_copy(gk, gk_hbm, store_sem.at[0])
    gk_store.start()

    def place(owner):
        return sum(((owner >> b) & 1) * (w >> (b + 1)) for b in range(levels))

    for j in range(w // 256):
        cols = pl.ds(j * 256, 256)
        res = dot(gb[:, :, cols].reshape(lb * ch, 256), mixed[...].reshape(lb * ch, w), 0, 0)
        for i in range(256 // owned):
            gf[pl.ds(place(j * (256 // owned) + i), owned), :] = res[i * owned:(i + 1) * owned]

    base = 0
    offset = 0
    halves = []

    def half_start(level, base, offset):
        size = w >> (level + 1)
        bit = lax.rem(lax.div(me, 1 << level), 2)
        keep = pl.multiple_of(base + bit * size, owned)
        give = pl.multiple_of(base + (1 - bit) * size, owned)

        @pl.loop(0, size // owned)
        def _(i):
            to = pl.multiple_of(offset + i * owned, owned)
            rs_send[pl.ds(to, owned), :] = gf[pl.ds(give + i * owned, owned), :].astype(BF)

        copy = pltpu.make_async_remote_copy(
            src_ref=rs_send.at[pl.ds(offset, size)], dst_ref=rs_recv.at[pl.ds(offset, size)],
            send_sem=rs_ssem.at[level], recv_sem=rs_rsem.at[level],
            device_id={"seq": me + (1 - 2 * bit) * (1 << level)}, device_id_type=MESH,
        )
        copy.start()
        halves.append(copy)
        return keep, offset + size

    def half_end(level, keep, offset):
        size = w >> (level + 1)
        halves[level].wait_recv()

        @pl.loop(0, size // owned)
        def _(i):
            at = pl.ds(pl.multiple_of(keep + i * owned, owned), owned)
            come = pl.ds(pl.multiple_of(offset - size + i * owned, owned), owned)
            gf[at, :] = gf[at, :] + rs_recv[come, :].astype(F32)

    base, offset = half_start(0, base, offset)

    @pl.loop(0, lb)
    def _(i):
        gmx = dot(gb[i], f[...], 1, 0)
        sig = jax.nn.sigmoid(g[i].astype(F32))
        gi[i] = (gmx * sig).astype(BF)
        gg[i] = (gmx * x[i].astype(F32) * sig * (1.0 - sig)).astype(BF)

    gi_store = pltpu.make_async_copy(gi, gi_hbm, store_sem.at[1])
    gi_store.start()
    gg_store = pltpu.make_async_copy(gg, gg_hbm, store_sem.at[2])
    gg_store.start()

    half_end(0, base, offset)
    base, offset = half_start(1, base, offset)

    own_k.wait()
    wait_in(2, mk)
    own_o = mix(3, kron, mk, oac, om, own_sem.at[3])

    half_end(1, base, offset)
    base, offset = half_start(2, base, offset)

    lanes = g2s.shape[2]
    g2s[...] = jnp.zeros_like(g2s)
    for j in range(steps):
        part_u = mu[pl.ds(j * 4 * lb, 4 * lb)].reshape(step_rows, pw)
        h = dot(part_u, mk[...].reshape(rows, pw), 1, 1)
        h = jnp.where(same_channel(), h, 0.0).reshape(4 * lb, CS, rows).sum(axis=1)
        h = dot(h, spread(0, rows, lanes), 1, 0, precision=lax.Precision.HIGHEST)
        for i in range(4):
            g2s[j * 4 + i, 0:lb, :] = h[i * lb:(i + 1) * lb]

    def g2_copy(d, s):
        return pltpu.make_async_remote_copy(
            src_ref=g2s.at[d], dst_ref=g2r.at[s],
            send_sem=g2_ssem.at[d], recv_sem=g2_rsem.at[s],
            device_id={"seq": d}, device_id_type=MESH,
        )

    @pl.loop(1, n)
    def _(j):
        d = lax.rem(me + j, n)
        g2_copy(d, me).start()

    g2r[pl.ds(me, 1)] = g2s[pl.ds(me, 1)]

    for level in range(2, levels):
        half_end(level, base, offset)
        if level + 1 < levels:
            base, offset = half_start(level + 1, base, offset)

    @pl.loop(1, n)
    def _(j):
        s = lax.rem(me + j, n)
        g2_copy(s, s).wait_recv()

    dpbuf[pl.ds(my_dp, 1)] = gf[pl.ds(base, owned), :].astype(BF)[None]
    g2dp[pl.ds(my_dp, 1)] = jnp.sum(g2r[...], axis=0, keepdims=True)

    def dp_copies(d, s):
        return [
            pltpu.make_async_remote_copy(
                src_ref=buf.at[s], dst_ref=buf.at[s],
                send_sem=dp_ssem.at[i, d], recv_sem=dp_rsem.at[i, s],
                device_id={"dp": d}, device_id_type=MESH,
            )
            for i, buf in enumerate((dpbuf, g2dp))
        ]

    for j in range(1, dps):
        for c in dp_copies(lax.rem(my_dp + j, dps), my_dp):
            c.start()
    for j in range(1, dps):
        s = lax.rem(my_dp + j, dps)
        for c in dp_copies(s, s):
            c.wait_recv()
    first = dpbuf[0].astype(F32)
    second = g2dp[0]
    for i in range(1, dps):
        first = first + dpbuf[i].astype(F32)
        second = second + g2dp[i]
    gf_ref[...] = first * (1.0 / math.sqrt(nb * ch * dps))
    gs_ref[...] = second[0:lb, 0:nb] * (1.0 / math.sqrt(ch * dps * w))

    own_o.wait()
    wait_back(3, om)
    out_store = pltpu.make_async_copy(om, out_hbm, store_sem.at[3])
    out_store.start()

    @pl.loop(1, n)
    def _(j):
        d = lax.rem(me + j, n)
        copy_to(0, share(u_hbm, d), part(mu, me), d, me).wait_send()
        copy_to(1, part(gac, d), share(gm, me), d, me).wait_send()
        copy_to(2, share(kern, d), part(mk, me), d, me).wait_send()
        copy_to(3, part(oac, d), share(om, me), d, me).wait_send()
        g2_copy(d, me).wait_send()

    for c in halves:
        c.wait_send()
    for j in range(1, dps):
        for c in dp_copies(lax.rem(my_dp + j, dps), my_dp):
            c.wait_send()
    gk_store.wait()
    gi_store.wait()
    gg_store.wait()
    out_store.wait()


def on_device(n, dps, inputs, gates, kernel, first_factor, second_factor, upstream):
    lb, ch, w = inputs.shape
    nb = second_factor.shape[0]
    pw = w // (n // (ch // CS))
    owned = w // n
    levels = n.bit_length() - 1
    lanes = max(nb, 128)
    act = jax.ShapeDtypeStruct((lb, ch, w), BF)
    a_act = pltpu.VMEM((lb, ch, w), BF)
    a_mov = pltpu.VMEM((nb, CS, pw), BF)
    hbm = pl.BlockSpec(memory_space=pl.ANY)
    vmem = pl.BlockSpec(memory_space=pltpu.VMEM)
    sem = pltpu.SemaphoreType.DMA
    flops = 6 * lb * ch * w * w
    return pl.pallas_call(
        functools.partial(layer_kernel, n, dps, lb, ch, w, nb),
        out_shape=(
            act, act, act, act,
            jax.ShapeDtypeStruct((owned, w), F32),
            jax.ShapeDtypeStruct((lb, nb), F32),
        ),
        in_specs=[hbm, hbm, hbm, hbm, vmem, hbm],
        out_specs=(hbm, hbm, hbm, hbm, vmem, vmem),
        scratch_shapes=[
            a_act, a_act, a_act, pltpu.VMEM((w, w), BF),
            a_act, a_act, a_act,
            a_mov, a_mov, a_mov, a_mov,
            a_act, a_act, a_act, a_act, a_act, a_act,
            pltpu.VMEM((nb * CS, nb * CS), BF), pltpu.VMEM((nb * CS, nb * CS), BF),
            pltpu.VMEM((w, w), F32),
            pltpu.VMEM((w, w), BF), pltpu.VMEM((w, w), BF),
            pltpu.VMEM((dps, owned, w), BF),
            pltpu.VMEM((n, 8, lanes), F32), pltpu.VMEM((n, 8, lanes), F32),
            pltpu.VMEM((dps, 8, lanes), F32),
            sem((4,)), sem((4,)), sem((4,)), sem((4, n)), sem((4, n)),
            sem((levels,)), sem((levels,)), sem((n,)), sem((n,)), sem((2, dps)), sem((2, dps)),
        ],
        compiler_params=pltpu.CompilerParams(
            collective_id=0, has_side_effects=True, vmem_limit_bytes=58 * 1024 * 1024
        ),
        cost_estimate=pl.CostEstimate(flops=flops, bytes_accessed=10 << 20, transcendentals=0),
    )(inputs, gates, kernel, first_factor, second_factor, upstream)


def solution(mesh):
    cut = P("seq", "dp", None)
    return jax.shard_map(
        functools.partial(on_device, mesh.shape["seq"], mesh.shape["dp"]),
        mesh=mesh,
        in_specs=(cut, cut, cut, P(), P(), cut),
        out_specs=(cut, cut, cut, cut, P("seq", None), P("seq", None)),
        check_vma=False,
    )
```

time: 282 us -> 128 us (0.45)
  Pallas kernels: 0 us -> 120 us
  blocking collectives: 112 us -> 0 us
  waiting for transfers between devices: 91.7 us -> 0 us
  local copies, waits for them, and re-layouts: 27.9 us -> 6.62 us
  matrix products: 18.1 us -> 0 us
  starting transfers between devices: 13.9 us -> 0 us
  between operations: 14.1 us -> 0.66 us
  other arithmetic: 3.93 us -> 0 us
    pallas_call x0 -> x1, Pallas kernels: none -> 120 us  [on_device(): pl.pallas_call(functools.partial(layer_kernel, n, dps, lb, ch, w, nb), ou...]
    psum x1 -> x0, waiting for transfers between devices: 69 us -> none  [on_device(): lax.psum((first_full, second_full), ('dp', 'seq'))]
    all_to_all x2 -> x0, blocking collectives: 62 us -> none  [the longest x1 32.1 us: on_device(): lax.all_to_all(up_rows, 'seq', split_axis=1, concat_axis=0, tiled=True)]
    psum x1 -> x0, blocking collectives: 50 us -> none  [on_device(): lax.psum((first_full, second_full), ('dp', 'seq'))]
    all_to_all x2 -> x0, waiting for transfers between devices: 22.6 us -> none  [the longest x1 22.6 us: on_device(): lax.all_to_all(kern_rows, 'seq', split_axis=1, concat_axis=0, tiled=True)]
    all_to_all x9 -> x0, local copies, waits for them, and re-layouts: 19.7 us -> none  [the longest x3 7.47 us: on_device(): lax.all_to_all(kern_rows, 'seq', split_axis=1, concat_axis=0, tiled=True)]
    dot_general x6 -> x0, matrix products: 18.1 us -> none  [the longest x1 5.66 us: on_device(): jnp.dot(flat_grad, first_factor, preferred_element_type=jnp.float32)]
    all_to_all x2 -> x0, starting transfers between devices: 13.9 us -> none  [the longest x1 8.83 us: on_device(): lax.all_to_all(across, 'seq', split_axis=0, concat_axis=1, tiled=True)]
  transfers between devices with their start and end apart: 3 -> 0, of which waited for: 2 -> 0; matrix products, arithmetic and copies ran while one was open for 4% -> 0% of each run, Pallas kernels for 0% -> 0%
where the time goes in v1:
time: 128 us; the launch traced here: 127 us
  Pallas kernels  120 us (94%)
  local copies, waits for them, and re-layouts  6.62 us (5%)
    pallas_call x1, Pallas kernels, on_device(): pl.pallas_call(functools.partial(layer_kernel, n, dps, lb, ch, w, nb), ou...  120 us
    unnamed x16, local copies, waits for them, and re-layouts  6.62 us

profile of v1, /device:TPU:0, one launch (start us, length us, event | category | flops | bytes accessed | tf_op | source)
XLA Modules:
  0.0 126.8 jit_solution(5202051993608045196)
XLA Ops:
  0.6 119.5 %shard_map.109 = (bf16[4,128,1024]{2,1,0:T(8,128)(2,1)}, bf16[4,128,1024]{2,1,0:T(8,128)(2,1)}, bf16[4,128,1024]{2,1,0:T(8,128)(2,1)}, bf16[4,128,1024]{2,1,0:T(...) custom-call(bf16[4,128,1024]{2,1,0:T(8,128)(2,1)} %x_hbm.1, bf16[4,128,1024]{2,1,0:T(8,128)(2,1)} %g_hbm.1, ...), custom_call_target="tpu_custom_call" | custom-call | flops 3221225472 | bytes 10485760 | tf_op jit(solution)/shard_map/pallas_call | solution.py:344
  120.2 0.0 copy-start.2
  120.2 0.0 copy-start.1
  120.2 2.4 %copy.18 = bf16[4,128,1024]{2,1,0:T(8,128)(2,1)} copy(bf16[4,128,1024]{2,1,0:T(8,128)(2,1)} %get-tuple-element.12) | data formatting | bytes 2097152
  122.6 0.0 copy-done.2
  122.6 0.0 copy-start
  122.6 1.0 copy.19
  123.6 0.0 copy-done.1
  123.6 0.0 copy-start.3
  123.6 0.0 copy-start.4
  123.6 1.0 copy.20
  124.6 0.0 copy-done
  124.6 1.0 copy.21
  125.5 0.0 copy-done.3
  125.5 0.7 copy.22
  126.2 0.0 copy-done.4
  126.2 0.6 copy.23
Async XLA Ops:
  120.2 2.4 %copy-start.2 = (bf16[4,128,1024]{2,1,0:T(8,128)(2,1)S(1)}, bf16[4,128,1024]{2,1,0:T(8,128)(2,1)}, u32[]{:S(2)}) copy-start(bf16[4,128,1024]{2,1,0:T(8,128)(2,1)} %get-tuple-element.13) | copy-start | bytes 3145732
  120.2 3.4 %copy-start.1 = (bf16[4,128,1024]{2,1,0:T(8,128)(2,1)S(1)}, bf16[4,128,1024]{2,1,0:T(8,128)(2,1)}, u32[]{:S(2)}) copy-start(bf16[4,128,1024]{2,1,0:T(8,128)(2,1)} %get-tuple-element.14) | copy-start | bytes 3145732
  122.6 2.0 %copy-start = (bf16[4,128,1024]{2,1,0:T(8,128)(2,1)S(1)}, bf16[4,128,1024]{2,1,0:T(8,128)(2,1)}, u32[]{:S(2)}) copy-start(bf16[4,128,1024]{2,1,0:T(8,128)(2,1)} %get-tuple-element.15) | copy-start | bytes 3145732
  123.6 1.9 %copy-start.3 = (f32[64,1024]{1,0:T(8,128)S(1)}, f32[64,1024]{1,0:T(8,128)}, u32[]{:S(2)}) copy-start(f32[64,1024]{1,0:T(8,128)} %get-tuple-element.16) | copy-start | bytes 786436
  123.6 2.7 %copy-start.4 = (f32[4,64]{1,0:T(4,128)S(1)}, f32[4,64]{1,0:T(4,128)}, u32[]{:S(2)}) copy-start(f32[4,64]{1,0:T(4,128)} %get-tuple-element.17) | copy-start | bytes 3076

commit v2 on v1

--- a/solution.py
+++ b/solution.py
@@ -37,10 +37,19 @@
     owned = w // n
     levels = n.bit_length() - 1
 
+    hw = pw // 2
+
     def share(ref, d):
         c0 = pl.multiple_of(lax.div(d, pg) * CS, CS)
         p0 = pl.multiple_of(lax.rem(d, pg) * pw, pw)
         return ref.at[:, pl.ds(c0, CS), pl.ds(p0, pw)]
+
+    def half_share(half, ref, d):
+        c0 = pl.multiple_of(lax.div(d, pg) * CS, CS)
+        p0 = pl.multiple_of(lax.rem(d, pg) * pw + half * hw, hw)
+        return ref.at[:, pl.ds(c0, CS), pl.ds(p0, hw)]
+
+    share_of = [functools.partial(half_share, i) for i in range(2)]
 
     def part(ref, d):
         return ref.at[pl.ds(d * lb, lb)]
@@ -114,28 +123,27 @@
             e = dot(a, spread(0, rows, nb).astype(BF), 1, 1)
             dst[pl.ds(r0, step_rows), :] = jnp.where(same_channel(), e, 0.0).astype(BF)
 
-    build(kron_t, 1)
-    build(kron, 0)
-
     def wait_in(phase, dst):
         @pl.loop(1, n)
         def _(j):
             s = lax.rem(me + j, n)
             copy_to(phase, part(dst, s), part(dst, s), s, s).wait_recv()
 
-    def wait_back(phase, dst):
+    def wait_back(phase, dst, share):
         @pl.loop(1, n)
         def _(j):
             s = lax.rem(me + j, n)
             copy_to(phase, share(dst, s), share(dst, s), s, s).wait_recv()
 
-    def mix(phase, matrix, src, acc, dst, sem):
+    def mix(phase, matrix, src, acc, dst, share, sem):
+        width = src.shape[2]
+
         @pl.loop(0, steps)
         def _(j):
             at = lax.rem(lax.div(me, 4) + j, steps)
             r0 = pl.multiple_of(at * step_rows, step_rows)
-            res = dot(matrix[pl.ds(r0, step_rows), :], src[...].reshape(rows, pw), 1, 0)
-            acc[pl.ds(at * 4 * lb, 4 * lb)] = res.astype(BF).reshape(4 * lb, CS, pw)
+            res = dot(matrix[pl.ds(r0, step_rows), :], src[...].reshape(rows, width), 1, 0)
+            acc[pl.ds(at * 4 * lb, 4 * lb)] = res.astype(BF).reshape(4 * lb, CS, width)
 
             @pl.loop(0, 4)
             def _(i):
@@ -149,20 +157,36 @@
         own.start()
         return own
 
+    def send_kern(half):
+        own = pltpu.make_async_copy(
+            share_of[half](kern, me), part(mk.at[half], me), own_sem.at[2 + half]
+        )
+        own.start()
+
+        @pl.loop(1, n)
+        def _(j):
+            d = lax.rem(me + j, n)
+            copy_to(2 + half, share_of[half](kern, d), part(mk.at[half], me), d, me).start()
+
+        return own
+
+    def mix_kern(half, own):
+        own.wait()
+        wait_in(2 + half, mk.at[half])
+        return mix(
+            4 + half, kron, mk.at[half], oac.at[half], om, share_of[half], own_sem.at[4 + half]
+        )
+
+    own_k0 = send_kern(0)
+    build(kron_t, 1)
+    build(kron, 0)
     own_u.wait()
     wait_in(0, mu)
-    own_g = mix(1, kron_t, mu, gac, gm, own_sem.at[1])
-
-    own_k = pltpu.make_async_copy(share(kern, me), part(mk, me), own_sem.at[2])
-    own_k.start()
-
-    @pl.loop(1, n)
-    def _(j):
-        d = lax.rem(me + j, n)
-        copy_to(2, share(kern, d), part(mk, me), d, me).start()
+    own_g = mix(1, kron_t, mu, gac, gm, share, own_sem.at[1])
+    own_k1 = send_kern(1)
 
     own_g.wait()
-    wait_back(1, gm)
+    wait_back(1, gm, share)
 
     @pl.loop(0, lb)
     def _(i):
@@ -217,6 +241,7 @@
             gf[at, :] = gf[at, :] + rs_recv[come, :].astype(F32)
 
     base, offset = half_start(0, base, offset)
+    own_o0 = mix_kern(0, own_k0)
 
     @pl.loop(0, lb)
     def _(i):
@@ -233,9 +258,7 @@
     half_end(0, base, offset)
     base, offset = half_start(1, base, offset)
 
-    own_k.wait()
-    wait_in(2, mk)
-    own_o = mix(3, kron, mk, oac, om, own_sem.at[3])
+    own_o1 = mix_kern(1, own_k1)
 
     half_end(1, base, offset)
     base, offset = half_start(2, base, offset)
@@ -244,7 +267,8 @@
     g2s[...] = jnp.zeros_like(g2s)
     for j in range(steps):
         part_u = mu[pl.ds(j * 4 * lb, 4 * lb)].reshape(step_rows, pw)
-        h = dot(part_u, mk[...].reshape(rows, pw), 1, 1)
+        h = dot(part_u[:, :hw], mk[0].reshape(rows, hw), 1, 1)
+        h = h + dot(part_u[:, hw:], mk[1].reshape(rows, hw), 1, 1)
         h = jnp.where(same_channel(), h, 0.0).reshape(4 * lb, CS, rows).sum(axis=1)
         h = dot(h, spread(0, rows, lanes), 1, 0, precision=lax.Precision.HIGHEST)
         for i in range(4):
@@ -302,8 +326,10 @@
     gf_ref[...] = first * (1.0 / math.sqrt(nb * ch * dps))
     gs_ref[...] = second[0:lb, 0:nb] * (1.0 / math.sqrt(ch * dps * w))
 
-    own_o.wait()
-    wait_back(3, om)
+    own_o0.wait()
+    own_o1.wait()
+    wait_back(4, om, share_of[0])
+    wait_back(5, om, share_of[1])
     out_store = pltpu.make_async_copy(om, out_hbm, store_sem.at[3])
     out_store.start()
 
@@ -312,8 +338,9 @@
         d = lax.rem(me + j, n)
         copy_to(0, share(u_hbm, d), part(mu, me), d, me).wait_send()
         copy_to(1, part(gac, d), share(gm, me), d, me).wait_send()
-        copy_to(2, share(kern, d), part(mk, me), d, me).wait_send()
-        copy_to(3, part(oac, d), share(om, me), d, me).wait_send()
+        for i in range(2):
+            copy_to(2 + i, share_of[i](kern, d), part(mk.at[i], me), d, me).wait_send()
+            copy_to(4 + i, part(oac.at[i], d), share_of[i](om, me), d, me).wait_send()
         g2_copy(d, me).wait_send()
 
     for c in halves:
@@ -325,6 +352,21 @@
     gi_store.wait()
     gg_store.wait()
     out_store.wait()
+
+
+def hand_over(*refs):
+    sems = refs[12]
+    copies = []
+    for i, (src, dst) in enumerate(zip(refs[:6], refs[6:12])):
+        if len(src.shape) == 3:
+            for j in range(src.shape[0]):
+                copies.append(pltpu.make_async_copy(src.at[j], dst.at[j], sems.at[i, j]))
+        else:
+            copies.append(pltpu.make_async_copy(src, dst, sems.at[i, 0]))
+    for c in copies:
+        c.start()
+    for c in copies:
+        c.wait()
 
 
 def on_device(n, dps, inputs, gates, kernel, first_factor, second_factor, upstream):
@@ -337,11 +379,12 @@
     act = jax.ShapeDtypeStruct((lb, ch, w), BF)
     a_act = pltpu.VMEM((lb, ch, w), BF)
     a_mov = pltpu.VMEM((nb, CS, pw), BF)
+    a_half = pltpu.VMEM((2, nb, CS, pw // 2), BF)
     hbm = pl.BlockSpec(memory_space=pl.ANY)
     vmem = pl.BlockSpec(memory_space=pltpu.VMEM)
     sem = pltpu.SemaphoreType.DMA
     flops = 6 * lb * ch * w * w
-    return pl.pallas_call(
+    results = pl.pallas_call(
         functools.partial(layer_kernel, n, dps, lb, ch, w, nb),
         out_shape=(
             act, act, act, act,
@@ -353,7 +396,7 @@
         scratch_shapes=[
             a_act, a_act, a_act, pltpu.VMEM((w, w), BF),
             a_act, a_act, a_act,
-            a_mov, a_mov, a_mov, a_mov,
+            a_mov, a_half, a_mov, a_half,
             a_act, a_act, a_act, a_act, a_act, a_act,
             pltpu.VMEM((nb * CS, nb * CS), BF), pltpu.VMEM((nb * CS, nb * CS), BF),
             pltpu.VMEM((w, w), F32),
@@ -361,7 +404,7 @@
             pltpu.VMEM((dps, owned, w), BF),
             pltpu.VMEM((n, 8, lanes), F32), pltpu.VMEM((n, 8, lanes), F32),
             pltpu.VMEM((dps, 8, lanes), F32),
-            sem((4,)), sem((4,)), sem((4,)), sem((4, n)), sem((4, n)),
+            sem((4,)), sem((6,)), sem((4,)), sem((6, n)), sem((6, n)),
             sem((levels,)), sem((levels,)), sem((n,)), sem((n,)), sem((2, dps)), sem((2, dps)),
         ],
         compiler_params=pltpu.CompilerParams(
@@ -369,6 +412,15 @@
         ),
         cost_estimate=pl.CostEstimate(flops=flops, bytes_accessed=10 << 20, transcendentals=0),
     )(inputs, gates, kernel, first_factor, second_factor, upstream)
+    return pl.pallas_call(
+        hand_over,
+        out_shape=tuple(jax.ShapeDtypeStruct(r.shape, r.dtype) for r in results),
+        in_specs=[hbm] * 6,
+        out_specs=(hbm,) * 6,
+        scratch_shapes=[sem((6, lb))],
+        compiler_params=pltpu.CompilerParams(vmem_limit_bytes=60 * 1024 * 1024),
+        cost_estimate=pl.CostEstimate(flops=0, bytes_accessed=8 << 20, transcendentals=0),
+    )(*results)
 
 
 def solution(mesh):

time: 128 us -> 264 us (2.06)
  Pallas kernels: 120 us -> 263 us
  local copies, waits for them, and re-layouts: 6.62 us -> 0 us
    pallas_call x0 -> x1, Pallas kernels: none -> 136 us  [on_device(): pl.pallas_call(hand_over, out_shape=tuple((jax.ShapeDtypeStruct(r.shape,...]
    pallas_call x1, Pallas kernels: 120 us -> 127 us  [on_device(): pl.pallas_call(functools.partial(layer_kernel, n, dps, lb, ch, w, nb), ou...]
    unnamed x16 -> x0, local copies, waits for them, and re-layouts: 6.62 us -> none
where the time goes in v2:
time: 264 us
  Pallas kernels  263 us (100%)
    pallas_call x1, Pallas kernels, on_device(): pl.pallas_call(hand_over, out_shape=tuple((jax.ShapeDtypeStruct(r.shape,...  136 us
    pallas_call x1, Pallas kernels, on_device(): pl.pallas_call(functools.partial(layer_kernel, n, dps, lb, ch, w, nb), ou...  127 us

profile of v2, /device:TPU:0, one launch (start us, length us, event | category | flops | bytes accessed | tf_op | source)
XLA Modules:
  0.0 263.8 jit_solution(12271731055935529410)
XLA Ops:
  0.6 126.8 %shard_map.109 = (bf16[4,128,1024]{2,1,0:T(8,128)(2,1)}, bf16[4,128,1024]{2,1,0:T(8,128)(2,1)}, bf16[4,128,1024]{2,1,0:T(8,128)(2,1)}, bf16[4,128,1024]{2,1,0:T(...) custom-call(bf16[4,128,1024]{2,1,0:T(8,128)(2,1)} %x_hbm.1, bf16[4,128,1024]{2,1,0:T(8,128)(2,1)} %g_hbm.1, ...), custom_call_target="tpu_custom_call" | custom-call | flops 3221225472 | bytes 10485760 | tf_op jit(solution)/shard_map/pallas_call | solution.py:387
  127.5 136.4 %shard_map.110 = (bf16[4,128,1024]{2,1,0:T(8,128)(2,1)}, bf16[4,128,1024]{2,1,0:T(8,128)(2,1)}, bf16[4,128,1024]{2,1,0:T(8,128)(2,1)}, bf16[4,128,1024]{2,1,0:T(...) custom-call(bf16[4,128,1024]{2,1,0:T(8,128)(2,1)} %get-tuple-element.12.refs_0_, ...), custom_call_target="tpu_custom_call" | custom-call | bytes 8388608 | tf_op jit(solution)/shard_map/pallas_call | solution.py:415

commit v3 on v1

--- a/solution.py
+++ b/solution.py
@@ -327,6 +327,11 @@
     out_store.wait()
 
 
+def hand_over(*refs):
+    for src, dst in zip(refs[:6], refs[6:]):
+        dst[...] = src[...]
+
+
 def on_device(n, dps, inputs, gates, kernel, first_factor, second_factor, upstream):
     lb, ch, w = inputs.shape
     nb = second_factor.shape[0]
@@ -341,7 +346,7 @@
     vmem = pl.BlockSpec(memory_space=pltpu.VMEM)
     sem = pltpu.SemaphoreType.DMA
     flops = 6 * lb * ch * w * w
-    return pl.pallas_call(
+    results = pl.pallas_call(
         functools.partial(layer_kernel, n, dps, lb, ch, w, nb),
         out_shape=(
             act, act, act, act,
@@ -369,6 +374,17 @@
         ),
         cost_estimate=pl.CostEstimate(flops=flops, bytes_accessed=10 << 20, transcendentals=0),
     )(inputs, gates, kernel, first_factor, second_factor, upstream)
+    block = pl.BlockSpec((1, ch, w), lambda i: (i, 0, 0))
+    specs = [block] * 4 + [pl.BlockSpec(r.shape, lambda i: (0, 0)) for r in results[4:]]
+    return pl.pallas_call(
+        hand_over,
+        grid=(lb,),
+        out_shape=tuple(jax.ShapeDtypeStruct(r.shape, r.dtype) for r in results),
+        in_specs=specs,
+        out_specs=tuple(specs),
+        compiler_params=pltpu.CompilerParams(vmem_limit_bytes=60 * 1024 * 1024),
+        cost_estimate=pl.CostEstimate(flops=0, bytes_accessed=8 << 20, transcendentals=0),
+    )(*results)
 
 
 def solution(mesh):

time: 128 us -> 126 us (0.984)
  local copies, waits for them, and re-layouts: 6.62 us -> 0 us
  Pallas kernels: 120 us -> 124 us
    unnamed x16 -> x0, local copies, waits for them, and re-layouts: 6.62 us -> none
    pallas_call x0 -> x1, Pallas kernels: none -> 4.91 us  [on_device(): pl.pallas_call(hand_over, grid=(lb,), out_shape=tuple((jax.ShapeDtypeStru...]
where the time goes in v3:
time: 126 us; the launch traced here: 125 us
  Pallas kernels  124 us (98%)
    pallas_call x1, Pallas kernels, on_device(): pl.pallas_call(functools.partial(layer_kernel, n, dps, lb, ch, w, nb), ou...  120 us
    pallas_call x1, Pallas kernels, on_device(): pl.pallas_call(hand_over, grid=(lb,), out_shape=tuple((jax.ShapeDtypeStru...  4.91 us

profile of v3, /device:TPU:0, one launch (start us, length us, event | category | flops | bytes accessed | tf_op | source)
XLA Modules:
  0.0 125.1 jit_solution(8789234096253673618)
XLA Ops:
  0.6 119.5 %shard_map.109 = (bf16[4,128,1024]{2,1,0:T(8,128)(2,1)}, bf16[4,128,1024]{2,1,0:T(8,128)(2,1)}, bf16[4,128,1024]{2,1,0:T(8,128)(2,1)}, bf16[4,128,1024]{2,1,0:T(...) custom-call(bf16[4,128,1024]{2,1,0:T(8,128)(2,1)} %x_hbm.1, bf16[4,128,1024]{2,1,0:T(8,128)(2,1)} %g_hbm.1, ...), custom_call_target="tpu_custom_call" | custom-call | flops 3221225472 | bytes 10485760 | tf_op jit(solution)/shard_map/pallas_call | solution.py:349
  120.2 4.9 %shard_map.110 = (bf16[4,128,1024]{2,1,0:T(8,128)(2,1)}, bf16[4,128,1024]{2,1,0:T(8,128)(2,1)}, bf16[4,128,1024]{2,1,0:T(8,128)(2,1)}, bf16[4,128,1024]{2,1,0:T(...) custom-call(bf16[4,128,1024]{2,1,0:T(8,128)(2,1)} %get-tuple-element.12.refs_0_, ...), custom_call_target="tpu_custom_call" | custom-call | bytes 8388608 | tf_op jit(solution)/shard_map/pallas_call | solution.py:379

commit v4 on v3

--- a/solution.py
+++ b/solution.py
@@ -233,12 +233,12 @@
     half_end(0, base, offset)
     base, offset = half_start(1, base, offset)
 
+    half_end(1, base, offset)
+    base, offset = half_start(2, base, offset)
+
     own_k.wait()
     wait_in(2, mk)
     own_o = mix(3, kron, mk, oac, om, own_sem.at[3])
-
-    half_end(1, base, offset)
-    base, offset = half_start(2, base, offset)
 
     lanes = g2s.shape[2]
     g2s[...] = jnp.zeros_like(g2s)

time: 126 us -> 135 us (1.071)
  Pallas kernels: 124 us -> 134 us
    pallas_call x1, Pallas kernels: 120 us -> 129 us  [on_device(): pl.pallas_call(functools.partial(layer_kernel, n, dps, lb, ch, w, nb), ou...]
where the time goes in v4:
time: 135 us
  Pallas kernels  134 us (99%)
    pallas_call x1, Pallas kernels, on_device(): pl.pallas_call(functools.partial(layer_kernel, n, dps, lb, ch, w, nb), ou...  129 us
    pallas_call x1, Pallas kernels, on_device(): pl.pallas_call(hand_over, grid=(lb,), out_shape=tuple((jax.ShapeDtypeStru...  4.91 us

profile of v4, /device:TPU:0, one launch (start us, length us, event | category | flops | bytes accessed | tf_op | source)
XLA Modules:
  0.0 134.9 jit_solution(551516423213589208)
XLA Ops:
  0.6 129.4 %shard_map.109 = (bf16[4,128,1024]{2,1,0:T(8,128)(2,1)}, bf16[4,128,1024]{2,1,0:T(8,128)(2,1)}, bf16[4,128,1024]{2,1,0:T(8,128)(2,1)}, bf16[4,128,1024]{2,1,0:T(...) custom-call(bf16[4,128,1024]{2,1,0:T(8,128)(2,1)} %x_hbm.1, bf16[4,128,1024]{2,1,0:T(8,128)(2,1)} %g_hbm.1, ...), custom_call_target="tpu_custom_call" | custom-call | flops 3221225472 | bytes 10485760 | tf_op jit(solution)/shard_map/pallas_call | solution.py:349
  130.0 4.9 %shard_map.110 = (bf16[4,128,1024]{2,1,0:T(8,128)(2,1)}, bf16[4,128,1024]{2,1,0:T(8,128)(2,1)}, bf16[4,128,1024]{2,1,0:T(8,128)(2,1)}, bf16[4,128,1024]{2,1,0:T(...) custom-call(bf16[4,128,1024]{2,1,0:T(8,128)(2,1)} %get-tuple-element.12.refs_0_, ...), custom_call_target="tpu_custom_call" | custom-call | bytes 8388608 | tf_op jit(solution)/shard_map/pallas_call | solution.py:379
